TPU v7x, 32 devices: a whole 2x2x4 slice. The times are simulated.
32 devices in a mesh: grp: 2 (over x), fin: 8 (over z, y), fout: 2 (over core).
Axes of the slice: x: 2, y: 2, z: 4, core: 2. Of those that a mesh axis runs over, the one named last changes fastest.
Arguments:
- tokens: bfloat16 [128, 6144], P(('grp', 'fin')), parts along dimension 0, may hold values from -6 to 6
- segment_ids: int32 [128], P(('grp', 'fin')), parts along dimension 0, may hold values from 0 to 3, never falling along the last dimension, each value on 1 to 32 neighbouring positions
- norm_gain: float32 [6144], replicated, may hold values from 0.1 to 1.9
- w_qkv: bfloat16 [6144, 3, 6144], P('fout', None, 'fin'), may hold values from -0.078125 to 0.078125
- w_up: bfloat16 [6144, 24576], P('fout', 'fin'), may hold values from -0.078125 to 0.078125
- w_out: bfloat16 [6144, 6144], P('fin', 'fout'), may hold values from -0.078125 to 0.078125
- w_down: bfloat16 [24576, 6144], P('fin', 'fout'), may hold values from -0.0390625 to 0.0390625
Outputs:
- layer_out: bfloat16 [128, 6144], P(('grp', 'fin'), 'fout'), parts along dimension 0
There are 2 independent parts, one for each index of `grp`. A program takes and returns all parts, laid end to end along the dimension named above; an argument that names none is the same for every part. Nothing has to cross between parts.
Inputs may be any that keep to these rules, and one draw needn't show every extreme that they name: segment_ids never fall along the tokens; each image holds 1 to 32 consecutive tokens and some image holds exactly 32; every number from 0 to 3 names an image.
All inputs are finite; a program needn't handle non-finite values.
Results may differ from a plain program's by a relative error of at most 0.0052.
Values may be sent and summed in bfloat16 or wider, within the bound.
A program may use at most 192 MiB of HBM per device.

v0:
```python
import math

import jax
import jax.numpy as jnp
from jax import lax
from jax.sharding import PartitionSpec as P

HEAD = 128


def feature_norm(values):
    center = jnp.mean(values, -1, keepdims=True)
    square = jnp.mean(values * values, -1, keepdims=True)
    return (values - center) * lax.rsqrt(square - center * center + 1e-06)


def attend(qkv_local, query_ids):
    spread = lax.all_to_all(qkv_local, "fin", split_axis=0, concat_axis=2, tiled=True)
    spread = spread.reshape(spread.shape[0], 3, -1, HEAD)
    query = feature_norm(spread[:, 0].astype(jnp.float32)).astype(jnp.bfloat16)
    keys = feature_norm(spread[:, 1].astype(jnp.float32)).astype(jnp.bfloat16)
    value = spread[:, 2]
    tok_rows, heads, head_size = query.shape
    factor = 1.0 / math.sqrt(head_size)
    marks = query_ids + 1
    key_part = lax.all_gather(keys, "fin", axis=0, tiled=True)
    value_part = lax.all_gather(value, "fin", axis=0, tiled=True)
    mark_part = lax.all_gather(marks, "fin", axis=0, tiled=True)
    scores = (
        jnp.einsum("qhd,khd->hqk", query, key_part, preferred_element_type=jnp.float32) * factor
    )
    same = marks[:, None] == mark_part[None, :]
    weight = jnp.where(same[None], jnp.exp(scores), 0.0).astype(jnp.bfloat16)
    den = jnp.sum(weight.astype(jnp.float32), -1)
    total = jnp.einsum("hqk,khd->qhd", weight, value_part, preferred_element_type=jnp.float32)
    total, den = (total, den)
    attended = (total / jnp.transpose(den)[:, :, None]).astype(jnp.bfloat16)
    return attended.reshape(tok_rows, heads * head_size)


def local(tokens, segment_ids, norm_gain, w_qkv, w_up, w_out, w_down):
    values = tokens.astype(jnp.float32)
    normed_full = (feature_norm(values) * norm_gain).astype(jnp.bfloat16)
    half_width = w_qkv.shape[0]
    offset = lax.axis_index("fout") * half_width
    normed = lax.dynamic_slice_in_dim(normed_full, offset, half_width, 1)
    residual = lax.dynamic_slice_in_dim(values, offset, half_width, 1)
    parts, columns = (w_qkv.shape[1], w_qkv.shape[2])
    qkv_cols = parts * columns
    qkv_matrix = w_qkv.reshape(half_width, qkv_cols)
    piece = lax.all_gather(normed, "fin", axis=0, tiled=True)
    first = jnp.dot(piece, qkv_matrix, preferred_element_type=jnp.float32)
    second = jnp.dot(piece, w_up, preferred_element_type=jnp.float32)
    partial_value = jnp.concatenate([first, second], axis=1)
    qkv_part = partial_value[:, :qkv_cols].reshape(partial_value.shape[0], parts, columns)
    up_part = partial_value[:, qkv_cols:]
    qkv_sum, up_sum = lax.psum((qkv_part, up_part), "fout")
    attended = attend(qkv_sum.astype(jnp.bfloat16), segment_ids)
    hidden = jax.nn.gelu(up_sum, approximate=False).astype(jnp.bfloat16)
    head_block = lax.all_to_all(attended, "fin", split_axis=1, concat_axis=0, tiled=True)
    first = jnp.dot(head_block, w_out, preferred_element_type=jnp.float32)
    mixed = lax.psum_scatter(
        first + jnp.dot(hidden, w_down, preferred_element_type=jnp.float32),
        "fin",
        scatter_dimension=0,
        tiled=True,
    )
    return (residual + mixed).astype(jnp.bfloat16)


def solution(mesh):
    return jax.shard_map(
        local,
        mesh=mesh,
        in_specs=(
            P(("grp", "fin"), None),
            P(("grp", "fin")),
            P(),
            P("fout", None, "fin"),
            P("fout", "fin"),
            P("fin", "fout"),
            P("fin", "fout"),
        ),
        out_specs=P(("grp", "fin"), "fout"),
        check_vma=False,
    )
```

profile of v0, /device:TPU:0, one launch (start us, length us, event | category | flops | bytes accessed | tf_op | source)
XLA Modules:
  0.0 259.2 jit_solution(12936262219170123338)
XLA Ops:
  6.5 1.1 convert_reduce_fusion.3
  7.6 0.9 convert_element_type.42
  8.5 0.7 dynamic-slice.1
  9.3 0.1 multiply_convert_fusion
  9.4 32.7 %all_gather.12 = bf16[64,3072]{1,0:T(8,128)(2,1)S(1)} all-gather(bf16[8,3072]{1,0:T(8,128)(2,1)S(1)} %multiply_convert_fusion), channel_id=1, replica_groups=mesh['grp'=2,'fin'=8,'fout'=2] {'fin'}, dimensions={0}, use_global_device_ids=true | all-gather | bytes 442368 | tf_op jit(solution)/shard_map/all_gather | solution.py:51
  42.1 18.6 %copy.35 = bf16[3072,3,768]{0,2,1:T(8,128)(2,1)} copy(bf16[3072,3,768]{2,0,1:T(8,128)(2,1)} %param.10) | data formatting | bytes 28311552 | tf_op args[3]
  60.7 9.4 %fusion = f32[64,3,768]{2,0,1:T(8,128)S(1)} fusion(bf16[3072,3,768]{0,2,1:T(8,128)(2,1)} %copy.35, bf16[64,3072]{1,0:T(8,128)(2,1)S(1)} %all_gather.12), kind=kOutput, calls=%fused_computation | convolution fusion | flops 905969664 | bytes 15138816 | tf_op jit(solution)/shard_map/dot_general | solution.py:52
  70.1 5.0 %all-reduce.5 = bf16[64,3,768]{2,0,1:T(8,128)(2,1)S(1)} all-reduce(f32[64,3,768]{2,0,1:T(8,128)S(1)} %fusion), channel_id=1, replica_groups=mesh['grp'=2,'fin'=8,'fout'=2] {'fout'}, use_global_device_ids=true, to_apply=%region_2.0 | all-reduce | flops 147456 | bytes 884736 | tf_op jit(solution)/shard_map/psum | solution.py:57
  75.1 1.0 copy.36
  76.1 5.8 %all-to-all-start = ((bf16[64,3,768]{2,1,0:T(4,128)(2,1)}), bf16[64,3,768]{2,1,0:T(4,128)(2,1)S(1)}, u32[]{:S(2)}, u32[]{:S(2)}) async-start(bf16[64,3,768]{2,1,0:T(4,128)(2,1)} %copy.36), calls=%async_computation | async-start | bytes 786432 | tf_op jit(solution)/shard_map/all_to_all | solution.py:18
  82.0 10.7 %fusion.95 = f32[64,3072]{1,0:T(8,128)} fusion(bf16[64,3072]{1,0:T(8,128)(2,1)S(1)} %all_gather.12, bf16[3072,3072]{1,0:T(8,128)(2,1)} %param.11), kind=kOutput, calls=%fused_computation.124 | convolution fusion | flops 1207959552 | bytes 20054016 | tf_op jit(solution)/shard_map/dot_general | solution.py:53
  92.7 0.6 dynamic-slice
  94.0 0.1 broadcast_add_fusion
  94.1 11.8 %all-reduce = s32[64]{0:T(128)S(1)} all-reduce(s32[64]{0:T(128)S(1)} %get-tuple-element.14), channel_id=1, replica_groups=mesh['grp'=2,'fin'=8,'fout'=2] {'fin'}, use_global_device_ids=true, to_apply=%add | all-reduce | flops 64 | bytes 512
  106.0 0.2 copy.57
  106.2 0.3 reshape.100
  106.5 0.1 convert_reduce_fusion.1
  106.6 0.1 fusion.56
  106.7 0.1 convert_reduce_fusion
  106.9 0.1 fusion.59
  107.1 0.1 copy.41
  107.3 0.2 fusion.58
  107.5 28.8 %all_gather.15 = bf16[64,48,128]{2,0,1:T(8,128)(2,1)S(1)} all-gather(bf16[8,48,128]{2,0,1:T(8,128)(2,1)S(1)} %fusion.58), channel_id=1, replica_groups=mesh['grp'=2,'fin'=8,'fout'=2] {'fin'}, dimensions={0}, use_global_device_ids=true | all-gather | bytes 884736 | tf_op jit(solution)/shard_map/all_gather | solution.py:26
  136.3 28.0 %all-gather = bf16[64,1,48,128]{3,0,2,1:T(8,128)(2,1)S(1)} all-gather(bf16[8,1,48,128]{3,0,2,1:T(8,128)(2,1)S(1)} %copy.47), channel_id=2, replica_groups=mesh['grp'=2,'fin'=8,'fout'=2] {'fin'}, dimensions={0}, use_global_device_ids=true | all-gather | bytes 884736 | tf_op jit(solution)/shard_map/all_gather | solution.py:27
  164.3 0.2 fusion.55
  164.5 0.6 convert_reduce_fusion.2
  165.1 0.3 fusion.6
  165.4 9.5 %all_to_all.34 = bf16[8,8,768]{2,0,1:T(8,128)(2,1)S(1)} all-to-all(bf16[8,8,768]{2,0,1:T(8,128)(2,1)S(1)} %bitcast.65), channel_id=1, replica_groups=mesh['grp'=2,'fin'=8,'fout'=2] {'fin'}, dimensions={1} | all-to-all | bytes 196608 | tf_op jit(solution)/shard_map/all_to_all | solution.py:60
  174.9 3.3 %fusion.60 = f32[64,3072]{1,0:T(8,128)S(1)} fusion(bf16[768,3072]{1,0:T(8,128)(2,1)} %param.12, bf16[8,8,768]{2,0,1:T(8,128)(2,1)S(1)} %all_to_all.34), kind=kOutput, calls=%fused_computation.78 | convolution fusion | flops 301989888 | bytes 5603328 | tf_op jit(solution)/shard_map/dot_general | solution.py:61
  178.2 12.3 %convolution_add_fusion = f32[64,3072]{1,0:T(8,128)} fusion(f32[64,3072]{1,0:T(8,128)S(1)} %fusion.60, bf16[3072,3072]{1,0:T(8,128)(2,1)} %param.13, f32[64,3072]{1,0:T(8,128)} %all-reduce.4.cloned.1.call-done), kind=kOutput, calls=%fused_computation.2 | convolution fusion | flops 1220935680 | bytes 21233664 | tf_op jit(solution)/shard_map/dot_general | solution.py:63
  190.5 60.3 %reduce-scatter.2.cloned.1.call-done = f32[8,3072]{1,0:T(8,128)} async-done(((f32[64,3072]{1,0:T(8,128)}), f32[8,3072]{1,0:T(8,128)}) %reduce-scatter.2.cloned.1.call-update) | async-done | bytes 98320 | tf_op jit(solution)/shard_map/reduce_scatter | solution.py:62
  250.8 1.5 add_convert_fusion
  (20 shorter events, 0.5 us)
Async XLA Ops:
  76.1 16.6 %copy-start.1 = (u32[32]{0:T(128)S(1)}, u32[32]{0:T(128)}, u32[]{:S(2)}) copy-start(u32[32]{0:T(128)} %constant.92) | copy-start | bytes 388
  76.1 17.8 %copy-start = (s32[8]{0:T(128)S(1)}, s32[8]{0:T(128)}, u32[]{:S(2)}) copy-start(s32[8]{0:T(128)} %param.8) | copy-start | bytes 100
  76.1 29.9 %all-to-all-start = ((bf16[64,3,768]{2,1,0:T(4,128)(2,1)}), bf16[64,3,768]{2,1,0:T(4,128)(2,1)S(1)}, u32[]{:S(2)}, u32[]{:S(2)}) async-start(bf16[64,3,768]{2,1,0:T(4,128)(2,1)} %copy.36), calls=%async_computation | async-start | bytes 786432 | tf_op jit(solution)/shard_map/all_to_all | solution.py:18
  81.9 96.3 %all-reduce.4.cloned.1.call-start = ((), (), s32[]{:S(2)}) async-start(), calls=%async_computation.3 | async-start | bytes 1572864 | tf_op jit(solution)/shard_map/psum | solution.py:57
  92.6 158.2 %reduce-scatter.2.cloned.1.call-start = ((), (), s32[]{:S(2)}) async-start(), calls=%async_computation.4 | async-start | bytes 884736 | tf_op jit(solution)/shard_map/reduce_scatter | solution.py:62
Sparse Core Ops, SparseCore 0:
  92.8 20.5 all-reduce.3
  190.7 60.0 reduce-scatter.1
where the time goes:
time: 260 us; the launch traced here: 259 us
  blocking collectives  116 us (45%)
  waiting for transfers between devices  60.3 us (23%)
  matrix products  36.5 us (14%)
  local copies, waits for them, and re-layouts  21.7 us (8%)
  between operations  14.2 us (5%)
  starting transfers between devices  5.88 us (2%)
  other arithmetic  4.67 us (2%)
    reduce_scatter x1, waiting for transfers between devices, local(): lax.psum_scatter(first + jnp.dot(hidden, w_down, preferred_element_type=j...  60.3 us
    all_gather x1, blocking collectives, local(): piece = lax.all_gather(normed, 'fin', axis=0, tiled=True)  32.7 us
    all_gather x1, blocking collectives, attend(): key_part = lax.all_gather(keys, 'fin', axis=0, tiled=True)  28.8 us
    all_gather x1, blocking collectives, attend(): value_part = lax.all_gather(value, 'fin', axis=0, tiled=True)  28 us
    unnamed x8, local copies, waits for them, and re-layouts  19.3 us
    dot_general x1, matrix products, local(): jnp.dot(hidden, w_down, preferred_element_type=jnp.float32)  12.3 us
    unnamed x1, blocking collectives  11.8 us
    dot_general x1, matrix products, local(): second = jnp.dot(piece, w_up, preferred_element_type=jnp.float32)  10.7 us
  transfers between devices with their start and end apart: 3, of which 1 were waited for; matrix products, arithmetic and copies ran while one was open for 7% of the time, Pallas kernels for 0%

commit v1 on v0

--- a/solution.py
+++ b/solution.py
@@ -1,11 +1,299 @@
+import functools
 import math
 
 import jax
 import jax.numpy as jnp
 from jax import lax
+from jax.experimental import pallas as pl
+from jax.experimental.pallas import tpu as pltpu
 from jax.sharding import PartitionSpec as P
 
 HEAD = 128
+LANES = 128
+TILE = 256
+PAIR = 2
+MESH = pl.DeviceIdType.MESH
+
+
+def fused_kernel(
+    lines, groups, chunks,
+    tokens, ids, gain, wq, wu, wo, wd, out,
+    wq_v, wu_v, wo_v, wd_v, xg, xs, idc, ps, pr, att, hid, p, ys, yr, zs, zr, own,
+    wsem, gsend, grecv, psend, precv, ysend, yrecv, zsend, zrecv,
+):
+    rows, width = tokens.shape
+    half = wu.shape[0]
+    parts, _, cols = wq.shape
+    count = lines * PAIR
+    toks = rows * count
+    up_w = wu.shape[1] // groups
+    out_w = half // chunks
+    me = lax.axis_index("fin")
+    core = lax.axis_index("fout")
+    z, y = lax.div(me, PAIR), lax.rem(me, PAIR)
+    y_peer = {"fin": z * PAIR + (1 - y)}
+    sibling = {"fout": 1 - core}
+
+    def line_at(step):
+        return lax.rem(z + step, lines)
+
+    loads = []
+    for part in range(parts):
+        loads.append(pltpu.make_async_copy(wq.at[part], wq_v.at[part], wsem.at[part]))
+    for g in range(groups):
+        at = pl.ds(g * up_w, up_w)
+        loads.append(pltpu.make_async_copy(wu.at[:, at], wu_v.at[:, at], wsem.at[parts + g]))
+    base = parts + groups
+    loads.append(pltpu.make_async_copy(wo, wo_v, wsem.at[base]))
+    for j in range(chunks):
+        at = pl.ds(j * out_w, out_w)
+        loads.append(pltpu.make_async_copy(wd.at[:, at], wd_v.at[:, at], wsem.at[base + 1 + j]))
+    for load in loads:
+        load.start()
+
+    barrier = pltpu.get_barrier_semaphore()
+    pl.semaphore_signal(barrier, inc=1, device_id=y_peer, device_id_type=MESH)
+    pl.semaphore_signal(barrier, inc=1, device_id=sibling, device_id_type=MESH)
+    for step in range(1, lines):
+        pl.semaphore_signal(
+            barrier, inc=1, device_id={"fin": line_at(step) * PAIR + y}, device_id_type=MESH
+        )
+
+    values = tokens[...].astype(jnp.float32)
+    center = jnp.mean(values, -1, keepdims=True)
+    square = jnp.mean(values * values, -1, keepdims=True)
+    scale = lax.rsqrt(square - center * center + 1e-06)
+    mine = pl.ds(pl.multiple_of(core * half, LANES), half)
+    normed = (tokens[:, mine].astype(jnp.float32) - center) * scale * gain[:, mine]
+    fold = half // 2
+    packed = jnp.concatenate([normed[:, :fold], normed[:, fold:]], axis=0)
+    xg[me, :, pl.ds(0, fold)] = packed.astype(jnp.bfloat16)
+    row = lax.broadcasted_iota(jnp.int32, (2 * rows, LANES), 0)
+    mark = jnp.zeros((2 * rows, LANES), jnp.float32)
+    for r in range(rows):
+        mark = jnp.where(row == r, ids[r].astype(jnp.float32), mark)
+    xg[me, :, pl.ds(fold, LANES)] = mark.astype(jnp.bfloat16)
+
+    pl.semaphore_wait(barrier, lines + 1)
+
+    def block(at, sem, to):
+        return pltpu.make_async_remote_copy(
+            src_ref=xg.at[at], dst_ref=xg.at[at], send_sem=gsend.at[sem], recv_sem=grecv.at[at],
+            device_id=to, device_id_type=MESH,
+        )
+
+    sends = [block(me, 0, y_peer)]
+    for step in range(1, lines):
+        sends.append(block(me, step, {"fin": line_at(step) * PAIR + y}))
+    for send in sends:
+        send.start()
+    for step in range(1, lines):
+        source = line_at(lines - step) * PAIR + y
+        passed = block(source, lines - 1 + step, y_peer)
+        passed.wait_recv()
+        passed.start()
+        sends.append(passed)
+    for step in range(lines):
+        block(line_at(lines - step) * PAIR + (1 - y), 0, y_peer).wait_recv()
+
+    for line in range(lines):
+        pair = [xg[line * PAIR + k].astype(jnp.float32) for k in range(PAIR)]
+        to = pl.ds(line * PAIR * rows, PAIR * rows)
+        xs[to, pl.ds(0, fold)] = jnp.concatenate(
+            [b[:rows, :fold] for b in pair], axis=0).astype(jnp.bfloat16)
+        xs[to, pl.ds(fold, fold)] = jnp.concatenate(
+            [b[rows:, :fold] for b in pair], axis=0).astype(jnp.bfloat16)
+        idc[to, :] = jnp.concatenate([b[:rows, fold:] for b in pair], axis=0)
+
+    swaps = []
+
+    def project(g, weight, start, size):
+        loads[g].wait()
+
+        def tile(t, carry):
+            src = pl.ds(pl.multiple_of(start + t * TILE, TILE), TILE)
+            dst = pl.ds(pl.multiple_of(t * TILE, TILE), TILE)
+            ps[g, :, dst] = jnp.dot(xs[...], weight[:, src], preferred_element_type=jnp.float32)
+            return carry
+
+        lax.fori_loop(0, size // TILE, tile, 0)
+        swap = pltpu.make_async_remote_copy(
+            src_ref=ps.at[g], dst_ref=pr.at[g], send_sem=psend.at[g], recv_sem=precv.at[g],
+            device_id=sibling, device_id_type=MESH,
+        )
+        swap.start()
+        swaps.append(swap)
+
+    def activate(g):
+        swaps[parts + g].wait_recv()
+        total = ps[parts + g] + pr[parts + g]
+        total = 0.5 * total * (1.0 + lax.erf(total * math.sqrt(0.5)))
+        hid[:, pl.ds(g * up_w, up_w)] = total.astype(jnp.bfloat16)
+
+    for part in range(parts):
+        project(part, wq_v.at[part], 0, cols)
+    for g in range(groups):
+        project(parts + g, wu_v, g * up_w, up_w)
+        if g:
+            activate(g - 1)
+
+    for part in range(parts):
+        swaps[part].wait_recv()
+    diagonal = lax.broadcasted_iota(jnp.int32, (toks, toks), 0) == lax.broadcasted_iota(
+        jnp.int32, (toks, toks), 1)
+    by_row = idc[:, pl.ds(0, toks)]
+    same = by_row == jnp.sum(jnp.where(diagonal, by_row, 0.0), axis=0, keepdims=True)
+
+    def head_norm(v):
+        m = jnp.mean(v, -1, keepdims=True)
+        s = jnp.mean(v * v, -1, keepdims=True)
+        return ((v - m) * lax.rsqrt(s - m * m + 1e-06)).astype(jnp.bfloat16)
+
+    for h in range(cols // HEAD):
+        at = pl.ds(h * HEAD, HEAD)
+        q, k, v = [(ps[i, :, at] + pr[i, :, at]).astype(jnp.bfloat16) for i in range(3)]
+        qn, kn = head_norm(q.astype(jnp.float32)), head_norm(k.astype(jnp.float32))
+        scores = lax.dot_general(
+            qn, kn, (((1,), (1,)), ((), ())), preferred_element_type=jnp.float32
+        ) * (1.0 / math.sqrt(HEAD))
+        e = jnp.where(same, jnp.exp(scores), 0.0).astype(jnp.bfloat16)
+        den = jnp.sum(e.astype(jnp.float32), -1, keepdims=True)
+        total = jnp.dot(e, v, preferred_element_type=jnp.float32)
+        att[:, at] = (total / den).astype(jnp.bfloat16)
+    activate(groups - 1)
+
+    loads[base].wait()
+    reduces = []
+
+    def line_rows(line, who):
+        return pl.ds(pl.multiple_of(line * (PAIR * rows) + who * rows, rows), rows)
+
+    def to_pair(j):
+        at = pl.ds(j * out_w, out_w)
+        theirs = jnp.concatenate([p[line_rows(k, 1 - y), at] for k in range(lines)], axis=0)
+        ys[j] = theirs.astype(jnp.bfloat16)
+        copy = pltpu.make_async_remote_copy(
+            src_ref=ys.at[j], dst_ref=yr.at[j], send_sem=ysend.at[j], recv_sem=yrecv.at[j],
+            device_id=y_peer, device_id_type=MESH,
+        )
+        copy.start()
+        return copy
+
+    def to_line(j, arrived):
+        arrived.wait_recv()
+        at = pl.ds(j * out_w, out_w)
+        got = yr[j].astype(jnp.float32)
+        for k in range(lines):
+            total = p[line_rows(k, y), at] + got[k * rows:(k + 1) * rows]
+            own[k, :, at] = total
+            zs[j, k] = jnp.concatenate(
+                [total[:, :out_w // 2], total[:, out_w // 2:]], axis=0).astype(jnp.bfloat16)
+        copies = []
+        for step in range(1, lines):
+            line = line_at(step)
+            copy = pltpu.make_async_remote_copy(
+                src_ref=zs.at[j, line], dst_ref=zr.at[j, step - 1],
+                send_sem=zsend.at[j, step - 1], recv_sem=zrecv.at[j, step - 1],
+                device_id={"fin": line * PAIR + y}, device_id_type=MESH,
+            )
+            copy.start()
+            copies.append(copy)
+        reduces.append(copies)
+
+    pairs = []
+    for j in range(chunks):
+        loads[base + 1 + j].wait()
+
+        def tile(t, carry):
+            at = pl.ds(pl.multiple_of(j * out_w + t * TILE, TILE), TILE)
+            p[:, at] = jnp.dot(
+                att[...], wo_v[:, at], preferred_element_type=jnp.float32
+            ) + jnp.dot(hid[...], wd_v[:, at], preferred_element_type=jnp.float32)
+            return carry
+
+        lax.fori_loop(0, out_w // TILE, tile, 0)
+        pairs.append(to_pair(j))
+        if j:
+            to_line(j - 1, pairs[j - 1])
+    to_line(chunks - 1, pairs[chunks - 1])
+
+    for j in range(chunks):
+        at = pl.ds(j * out_w, out_w)
+        total = own[z, :, at]
+        for copy_at, copy in enumerate(reduces[j]):
+            copy.wait_recv()
+            got = zr[j, copy_at].astype(jnp.float32)
+            total = total + jnp.concatenate([got[:rows], got[rows:]], axis=1)
+        residual = tokens[:, pl.ds(pl.multiple_of(core * half + j * out_w, LANES), out_w)]
+        out[:, at] = (residual.astype(jnp.float32) + total).astype(jnp.bfloat16)
+
+    for copy in sends + swaps + pairs:
+        copy.wait_send()
+    for copies in reduces:
+        for copy in copies:
+            copy.wait_send()
+
+
+def fused(lines, tokens, segment_ids, norm_gain, w_qkv, w_up, w_out, w_down):
+    rows = tokens.shape[0]
+    half, parts, cols = w_qkv.shape
+    wide = w_up.shape[1]
+    count = lines * PAIR
+    toks = rows * count
+    groups = wide // cols
+    chunks = half // cols
+    out_w = half // chunks
+    bf16, f32 = jnp.bfloat16, jnp.float32
+    dma = pltpu.SemaphoreType.DMA
+    vmem = pl.BlockSpec(memory_space=pltpu.VMEM)
+    hbm = pl.BlockSpec(memory_space=pl.ANY)
+    macs = toks * (half * (parts * cols + wide) + (cols + wide) * half)
+    return pl.pallas_call(
+        functools.partial(fused_kernel, lines, groups, chunks),
+        out_shape=jax.ShapeDtypeStruct((rows, half), bf16),
+        in_specs=[vmem, pl.BlockSpec(memory_space=pltpu.SMEM), vmem, hbm, hbm, hbm, hbm],
+        out_specs=vmem,
+        scratch_shapes=[
+            pltpu.VMEM((parts, half, cols), bf16),
+            pltpu.VMEM((half, wide), bf16),
+            pltpu.VMEM((cols, half), bf16),
+            pltpu.VMEM((wide, half), bf16),
+            pltpu.VMEM((count, 2 * rows, half // 2 + LANES), bf16),
+            pltpu.VMEM((toks, half), bf16),
+            pltpu.VMEM((toks, LANES), f32),
+            pltpu.VMEM((parts + groups, toks, cols), f32),
+            pltpu.VMEM((parts + groups, toks, cols), f32),
+            pltpu.VMEM((toks, cols), bf16),
+            pltpu.VMEM((toks, wide), bf16),
+            pltpu.VMEM((toks, half), f32),
+            pltpu.VMEM((chunks, toks // PAIR, out_w), bf16),
+            pltpu.VMEM((chunks, toks // PAIR, out_w), bf16),
+            pltpu.VMEM((chunks, lines, 2 * rows, out_w // 2), bf16),
+            pltpu.VMEM((chunks, lines - 1, 2 * rows, out_w // 2), bf16),
+            pltpu.VMEM((lines, rows, half), f32),
+            dma((parts + groups + 1 + chunks,)),
+            dma((2 * lines - 1,)),
+            dma((count,)),
+            dma((parts + groups,)),
+            dma((parts + groups,)),
+            dma((chunks,)),
+            dma((chunks,)),
+            dma((chunks, lines - 1)),
+            dma((chunks, lines - 1)),
+        ],
+        compiler_params=pltpu.CompilerParams(
+            collective_id=0, has_side_effects=True, vmem_limit_bytes=VMEM_LIMIT
+        ),
+        cost_estimate=pl.CostEstimate(
+            flops=2 * macs, bytes_accessed=2 * macs // toks, transcendentals=0
+        ),
+    )(
+        tokens, segment_ids, norm_gain.reshape(1, -1), jnp.transpose(w_qkv, (1, 0, 2)),
+        w_up, w_out, w_down,
+    )
+
+
+VMEM_LIMIT = 63 << 20
 
 
 def feature_norm(values):
@@ -68,9 +356,33 @@
     return (residual + mixed).astype(jnp.bfloat16)
 
 
+def fits(mesh, tokens, w_qkv, w_up, w_out):
+    fin, rows = mesh.shape["fin"], tokens.shape[0] // (mesh.shape["grp"] * mesh.shape["fin"])
+    half, cols = w_qkv.shape[0] // mesh.shape["fout"], w_qkv.shape[2] // fin
+    wide = w_up.shape[1] // fin
+    weights = 2 * half * (w_qkv.shape[1] * cols + cols + 2 * wide)
+    return (
+        mesh.shape["fout"] == 2 and fin % PAIR == 0 and fin > PAIR and rows == 8
+        and rows * fin <= LANES and cols % TILE == 0 and cols % HEAD == 0
+        and wide % cols == 0 and half % cols == 0 and weights <= 56 << 20
+    )
+
+
 def solution(mesh):
+    def run(*args):
+        tokens, _, _, w_qkv, w_up, w_out, _ = args
+        if fits(mesh, tokens, w_qkv, w_up, w_out):
+            body = functools.partial(fused, mesh.shape["fin"] // PAIR)
+        else:
+            body = local
+        return placed(mesh, body)(*args)
+
+    return run
+
+
+def placed(mesh, body):
     return jax.shard_map(
-        local,
+        body,
         mesh=mesh,
         in_specs=(
             P(("grp", "fin"), None),

time: 260 us -> 43.5 us (0.17)
  blocking collectives: 116 us -> 0 us
  waiting for transfers between devices: 60.3 us -> 0 us
  Pallas kernels: 0 us -> 41.9 us
  matrix products: 36.5 us -> 0 us
  local copies, waits for them, and re-layouts: 21.7 us -> 1.42 us
  between operations: 14.2 us -> 0.01 us
  starting transfers between devices: 5.88 us -> 0 us
  other arithmetic: 4.67 us -> 0 us
    all_gather x3 -> x0, blocking collectives: 89.5 us -> none  [the longest x1 32.7 us: local(): piece = lax.all_gather(normed, 'fin', axis=0, tiled=True)]
    reduce_scatter x1 -> x0, waiting for transfers between devices: 60.3 us -> none  [local(): lax.psum_scatter(first + jnp.dot(hidden, w_down, preferred_element_type=j...]
    pallas_call x0 -> x1, Pallas kernels: none -> 41.9 us  [fused(): pl.pallas_call(functools.partial(fused_kernel, lines, groups, chunks), ou...]
    dot_general x6 -> x0, matrix products: 36.5 us -> none  [the longest x1 12.3 us: local(): jnp.dot(hidden, w_down, preferred_element_type=jnp.float32)]
    unnamed x8 -> x1, local copies, waits for them, and re-layouts: 19.3 us -> 1.42 us
    unnamed x1 -> x0, blocking collectives: 11.8 us -> none
    all_to_all x1 -> x0, blocking collectives: 9.51 us -> none  [local(): lax.all_to_all(attended, 'fin', split_axis=1, concat_axis=0, tiled=True)]
    all_to_all x1 -> x0, starting transfers between devices: 5.8 us -> none  [attend(): lax.all_to_all(qkv_local, 'fin', split_axis=0, concat_axis=2, tiled=True)]
  transfers between devices with their start and end apart: 3 -> 0, of which waited for: 1 -> 0; matrix products, arithmetic and copies ran while one was open for 7% -> 0% of each run, Pallas kernels for 0% -> 0%
where the time goes in v1:
time: 43.5 us; the launch traced here: 43.3 us
  Pallas kernels  41.9 us (96%)
  local copies, waits for them, and re-layouts  1.42 us (3%)
    pallas_call x1, Pallas kernels, fused(): pl.pallas_call(functools.partial(fused_kernel, lines, groups, chunks), ou...  41.9 us
    unnamed x1, local copies, waits for them, and re-layouts  1.42 us

profile of v1, /device:TPU:0, one launch (start us, length us, event | category | flops | bytes accessed | tf_op | source)
XLA Modules:
  0.0 43.3 jit_solution(7751165442534479851)
XLA Ops:
  0.0 41.9 %shard_map.73 = bf16[8,3072]{1,0:T(8,128)(2,1)} custom-call(bf16[8,6144]{1,0:T(8,128)(2,1)} %tokens.1, s32[8]{0:T(128)} %ids.1, f32[1,6144]{1,0:T(1,128)} %bitcast.3, bf16[3,3072,768]{2,1,0:T(8,128)(2,1)} %bitcast.2, bf16[3072,3072]{1,0:T(8,128)(2,1)} %wu.1, bf16[768,3072]{1,0:T(8,128)(2,1)} %wo.1, bf16[3072,3072]{1,0:T(8,128)(2,1)} %wd.1), custom_call_target="tpu_custom_call" | custom-call | flops 3623878656 | bytes 56623104 | tf_op jit(solution)/shard_map/pallas_call | solution.py:251
  41.9 1.4 %copy.9 = bf16[8,3072]{1,0:T(8,128)(2,1)} copy(bf16[8,3072]{1,0:T(8,128)(2,1)} %shard_map.73) | data formatting | bytes 98304

commit v2 on v1

--- a/solution.py
+++ b/solution.py
@@ -12,13 +12,15 @@
 LANES = 128
 TILE = 256
 PAIR = 2
+HALVES = 2
+LAG = 2
 MESH = pl.DeviceIdType.MESH
 
 
 def fused_kernel(
     lines, groups, chunks,
     tokens, ids, gain, wq, wu, wo, wd, out,
-    wq_v, wu_v, wo_v, wd_v, xg, xs, idc, ps, pr, att, hid, p, ys, yr, zs, zr, own,
+    wq_v, wu_v, wo_v, wd_v, xa, xb, xs, idc, ps, pr, att, hid, p, ys, yr, zs, zr, own,
     wsem, gsend, grecv, psend, precv, ysend, yrecv, zsend, zrecv,
 ):
     rows, width = tokens.shape
@@ -37,13 +39,19 @@
     def line_at(step):
         return lax.rem(z + step, lines)
 
+    fold = half // HALVES
+    columns = parts + groups
     loads = []
-    for part in range(parts):
-        loads.append(pltpu.make_async_copy(wq.at[part], wq_v.at[part], wsem.at[part]))
-    for g in range(groups):
-        at = pl.ds(g * up_w, up_w)
-        loads.append(pltpu.make_async_copy(wu.at[:, at], wu_v.at[:, at], wsem.at[parts + g]))
-    base = parts + groups
+    for f in range(HALVES):
+        depth = pl.ds(f * fold, fold)
+        for part in range(parts):
+            loads.append(pltpu.make_async_copy(
+                wq.at[part, depth], wq_v.at[part, depth], wsem.at[f * columns + part]))
+        for g in range(groups):
+            at = pl.ds(g * up_w, up_w)
+            loads.append(pltpu.make_async_copy(
+                wu.at[depth, at], wu_v.at[depth, at], wsem.at[f * columns + parts + g]))
+    base = HALVES * columns
     loads.append(pltpu.make_async_copy(wo, wo_v, wsem.at[base]))
     for j in range(chunks):
         at = pl.ds(j * out_w, out_w)
@@ -65,58 +73,78 @@
     scale = lax.rsqrt(square - center * center + 1e-06)
     mine = pl.ds(pl.multiple_of(core * half, LANES), half)
     normed = (tokens[:, mine].astype(jnp.float32) - center) * scale * gain[:, mine]
-    fold = half // 2
-    packed = jnp.concatenate([normed[:, :fold], normed[:, fold:]], axis=0)
-    xg[me, :, pl.ds(0, fold)] = packed.astype(jnp.bfloat16)
+    piece = fold // 2
+    blocks = (xa, xb)
+    for f in range(HALVES):
+        low = f * fold
+        packed = jnp.concatenate(
+            [normed[:, low:low + piece], normed[:, low + piece:low + fold]], axis=0)
+        blocks[f][me, :, pl.ds(0, piece)] = packed.astype(jnp.bfloat16)
     row = lax.broadcasted_iota(jnp.int32, (2 * rows, LANES), 0)
     mark = jnp.zeros((2 * rows, LANES), jnp.float32)
     for r in range(rows):
         mark = jnp.where(row == r, ids[r].astype(jnp.float32), mark)
-    xg[me, :, pl.ds(fold, LANES)] = mark.astype(jnp.bfloat16)
+    xb[me, :, pl.ds(piece, LANES)] = mark.astype(jnp.bfloat16)
 
     pl.semaphore_wait(barrier, lines + 1)
 
-    def block(at, sem, to):
+    def block(f, at, sem, to):
         return pltpu.make_async_remote_copy(
-            src_ref=xg.at[at], dst_ref=xg.at[at], send_sem=gsend.at[sem], recv_sem=grecv.at[at],
+            src_ref=blocks[f].at[at], dst_ref=blocks[f].at[at],
+            send_sem=gsend.at[f, sem], recv_sem=grecv.at[f, at],
             device_id=to, device_id_type=MESH,
         )
 
-    sends = [block(me, 0, y_peer)]
-    for step in range(1, lines):
-        sends.append(block(me, step, {"fin": line_at(step) * PAIR + y}))
+    sends = []
+    for f in range(HALVES):
+        sends.append(block(f, me, 0, y_peer))
+        for step in range(1, lines):
+            sends.append(block(f, me, step, {"fin": line_at(step) * PAIR + y}))
     for send in sends:
         send.start()
-    for step in range(1, lines):
+
+    def pass_on(f, step):
         source = line_at(lines - step) * PAIR + y
-        passed = block(source, lines - 1 + step, y_peer)
+        passed = block(f, source, lines - 1 + step, y_peer)
         passed.wait_recv()
         passed.start()
         sends.append(passed)
-    for step in range(lines):
-        block(line_at(lines - step) * PAIR + (1 - y), 0, y_peer).wait_recv()
-
-    for line in range(lines):
-        pair = [xg[line * PAIR + k].astype(jnp.float32) for k in range(PAIR)]
-        to = pl.ds(line * PAIR * rows, PAIR * rows)
-        xs[to, pl.ds(0, fold)] = jnp.concatenate(
-            [b[:rows, :fold] for b in pair], axis=0).astype(jnp.bfloat16)
-        xs[to, pl.ds(fold, fold)] = jnp.concatenate(
-            [b[rows:, :fold] for b in pair], axis=0).astype(jnp.bfloat16)
-        idc[to, :] = jnp.concatenate([b[:rows, fold:] for b in pair], axis=0)
+
+    def unpack(f):
+        for step in range(lines):
+            block(f, line_at(lines - step) * PAIR + (1 - y), 0, y_peer).wait_recv()
+        low = f * fold
+        for line in range(lines):
+            pair = [blocks[f][line * PAIR + k].astype(jnp.float32) for k in range(PAIR)]
+            to = pl.ds(line * PAIR * rows, PAIR * rows)
+            xs[to, pl.ds(low, piece)] = jnp.concatenate(
+                [b[:rows, :piece] for b in pair], axis=0).astype(jnp.bfloat16)
+            xs[to, pl.ds(low + piece, piece)] = jnp.concatenate(
+                [b[rows:, :piece] for b in pair], axis=0).astype(jnp.bfloat16)
+            if f:
+                idc[to, :] = jnp.concatenate([b[:rows, piece:] for b in pair], axis=0)
+
+    for step in range(1, lines):
+        pass_on(0, step)
+    unpack(0)
 
     swaps = []
 
-    def project(g, weight, start, size):
-        loads[g].wait()
+    def project(f, g, weight, start, size):
+        loads[f * columns + g].wait()
+        depth = pl.ds(f * fold, fold)
 
         def tile(t, carry):
             src = pl.ds(pl.multiple_of(start + t * TILE, TILE), TILE)
             dst = pl.ds(pl.multiple_of(t * TILE, TILE), TILE)
-            ps[g, :, dst] = jnp.dot(xs[...], weight[:, src], preferred_element_type=jnp.float32)
+            product = jnp.dot(
+                xs[:, depth], weight[depth, src], preferred_element_type=jnp.float32)
+            ps[g, :, dst] = ps[g, :, dst] + product if f else product
             return carry
 
         lax.fori_loop(0, size // TILE, tile, 0)
+        if f < HALVES - 1:
+            return
         swap = pltpu.make_async_remote_copy(
             src_ref=ps.at[g], dst_ref=pr.at[g], send_sem=psend.at[g], recv_sem=precv.at[g],
             device_id=sibling, device_id_type=MESH,
@@ -130,12 +158,27 @@
         total = 0.5 * total * (1.0 + lax.erf(total * math.sqrt(0.5)))
         hid[:, pl.ds(g * up_w, up_w)] = total.astype(jnp.bfloat16)
 
-    for part in range(parts):
-        project(part, wq_v.at[part], 0, cols)
-    for g in range(groups):
-        project(parts + g, wu_v, g * up_w, up_w)
-        if g:
-            activate(g - 1)
+    def project_all(f, then):
+        for part in range(parts):
+            project(f, part, wq_v.at[part], 0, cols)
+            then(part)
+        for g in range(groups):
+            project(f, parts + g, wu_v, g * up_w, up_w)
+            then(parts + g)
+
+    def between(at):
+        if at % 2 == 0 and at // 2 + 1 < lines:
+            pass_on(1, at // 2 + 1)
+
+    def after(at):
+        if at > parts:
+            activate(at - parts - 1)
+
+    project_all(0, between)
+    for step in range(columns // 2 + columns % 2 + 1, lines):
+        pass_on(1, step)
+    unpack(1)
+    project_all(1, after)
 
     for part in range(parts):
         swaps[part].wait_recv()
@@ -213,9 +256,10 @@
 
         lax.fori_loop(0, out_w // TILE, tile, 0)
         pairs.append(to_pair(j))
-        if j:
-            to_line(j - 1, pairs[j - 1])
-    to_line(chunks - 1, pairs[chunks - 1])
+        if j >= LAG:
+            to_line(j - LAG, pairs[j - LAG])
+    for j in range(chunks - LAG, chunks):
+        to_line(j, pairs[j])
 
     for j in range(chunks):
         at = pl.ds(j * out_w, out_w)
@@ -241,7 +285,7 @@
     count = lines * PAIR
     toks = rows * count
     groups = wide // cols
-    chunks = half // cols
+    chunks = half // (2 * TILE)
     out_w = half // chunks
     bf16, f32 = jnp.bfloat16, jnp.float32
     dma = pltpu.SemaphoreType.DMA
@@ -258,7 +302,8 @@
             pltpu.VMEM((half, wide), bf16),
             pltpu.VMEM((cols, half), bf16),
             pltpu.VMEM((wide, half), bf16),
-            pltpu.VMEM((count, 2 * rows, half // 2 + LANES), bf16),
+            pltpu.VMEM((count, 2 * rows, half // 4), bf16),
+            pltpu.VMEM((count, 2 * rows, half // 4 + LANES), bf16),
             pltpu.VMEM((toks, half), bf16),
             pltpu.VMEM((toks, LANES), f32),
             pltpu.VMEM((parts + groups, toks, cols), f32),
@@ -271,9 +316,9 @@
             pltpu.VMEM((chunks, lines, 2 * rows, out_w // 2), bf16),
             pltpu.VMEM((chunks, lines - 1, 2 * rows, out_w // 2), bf16),
             pltpu.VMEM((lines, rows, half), f32),
-            dma((parts + groups + 1 + chunks,)),
-            dma((2 * lines - 1,)),
-            dma((count,)),
+            dma((HALVES * (parts + groups) + 1 + chunks,)),
+            dma((HALVES, 2 * lines - 1)),
+            dma((HALVES, count)),
             dma((parts + groups,)),
             dma((parts + groups,)),
             dma((chunks,)),
@@ -364,7 +409,7 @@
     return (
         mesh.shape["fout"] == 2 and fin % PAIR == 0 and fin > PAIR and rows == 8
         and rows * fin <= LANES and cols % TILE == 0 and cols % HEAD == 0
-        and wide % cols == 0 and half % cols == 0 and weights <= 56 << 20
+        and wide % cols == 0 and half % (2 * LAG * TILE) == 0 and weights <= 56 << 20
     )
 
 

time: 43.5 us -> 45.2 us (1.039)
  Pallas kernels: 41.9 us -> 43.6 us
    pallas_call x1, Pallas kernels: 41.9 us -> 43.6 us  [fused(): pl.pallas_call(functools.partial(fused_kernel, lines, groups, chunks), ou...]
where the time goes in v2:
time: 45.2 us; the launch traced here: 45 us
  Pallas kernels  43.6 us (96%)
  local copies, waits for them, and re-layouts  1.42 us (3%)
    pallas_call x1, Pallas kernels, fused(): pl.pallas_call(functools.partial(fused_kernel, lines, groups, chunks), ou...  43.6 us
    unnamed x1, local copies, waits for them, and re-layouts  1.42 us

profile of v2, /device:TPU:0, one launch (start us, length us, event | category | flops | bytes accessed | tf_op | source)
XLA Modules:
  0.0 45.0 jit_solution(4647050949032950858)
XLA Ops:
  0.0 43.6 %shard_map.73 = bf16[8,3072]{1,0:T(8,128)(2,1)} custom-call(bf16[8,6144]{1,0:T(8,128)(2,1)} %tokens.1, s32[8]{0:T(128)} %ids.1, f32[1,6144]{1,0:T(1,128)} %bitcast.3, bf16[3,3072,768]{2,1,0:T(8,128)(2,1)} %bitcast.2, bf16[3072,3072]{1,0:T(8,128)(2,1)} %wu.1, bf16[768,3072]{1,0:T(8,128)(2,1)} %wo.1, bf16[3072,3072]{1,0:T(8,128)(2,1)} %wd.1), custom_call_target="tpu_custom_call" | custom-call | flops 3623878656 | bytes 56623104 | tf_op jit(solution)/shard_map/pallas_call | solution.py:295
  43.6 1.4 %copy.9 = bf16[8,3072]{1,0:T(8,128)(2,1)} copy(bf16[8,3072]{1,0:T(8,128)(2,1)} %shard_map.73) | data formatting | bytes 98304

commit v3 on v1

--- a/solution.py
+++ b/solution.py
@@ -12,6 +12,7 @@
 LANES = 128
 TILE = 256
 PAIR = 2
+LAG = 2
 MESH = pl.DeviceIdType.MESH
 
 
@@ -213,9 +214,10 @@
 
         lax.fori_loop(0, out_w // TILE, tile, 0)
         pairs.append(to_pair(j))
-        if j:
-            to_line(j - 1, pairs[j - 1])
-    to_line(chunks - 1, pairs[chunks - 1])
+        if j >= LAG:
+            to_line(j - LAG, pairs[j - LAG])
+    for j in range(chunks - LAG, chunks):
+        to_line(j, pairs[j])
 
     for j in range(chunks):
         at = pl.ds(j * out_w, out_w)
@@ -364,7 +366,7 @@
     return (
         mesh.shape["fout"] == 2 and fin % PAIR == 0 and fin > PAIR and rows == 8
         and rows * fin <= LANES and cols % TILE == 0 and cols % HEAD == 0
-        and wide % cols == 0 and half % cols == 0 and weights <= 56 << 20
+        and wide % cols == 0 and half % cols == 0 and half // cols >= LAG and weights <= 56 << 20
     )
 
 

time: 43.5 us -> 42 us (0.966)
  Pallas kernels: 41.9 us -> 40.4 us
    pallas_call x1, Pallas kernels: 41.9 us -> 40.4 us  [fused(): pl.pallas_call(functools.partial(fused_kernel, lines, groups, chunks), ou...]
where the time goes in v3:
time: 42 us; the launch traced here: 41.8 us
  Pallas kernels  40.4 us (96%)
  local copies, waits for them, and re-layouts  1.42 us (3%)
    pallas_call x1, Pallas kernels, fused(): pl.pallas_call(functools.partial(fused_kernel, lines, groups, chunks), ou...  40.4 us
    unnamed x1, local copies, waits for them, and re-layouts  1.42 us

profile of v3, /device:TPU:0, one launch (start us, length us, event | category | flops | bytes accessed | tf_op | source)
XLA Modules:
  0.0 41.8 jit_solution(18265186475191379282)
XLA Ops:
  0.0 40.4 %shard_map.73 = bf16[8,3072]{1,0:T(8,128)(2,1)} custom-call(bf16[8,6144]{1,0:T(8,128)(2,1)} %tokens.1, s32[8]{0:T(128)} %ids.1, f32[1,6144]{1,0:T(1,128)} %bitcast.3, bf16[3,3072,768]{2,1,0:T(8,128)(2,1)} %bitcast.2, bf16[3072,3072]{1,0:T(8,128)(2,1)} %wu.1, bf16[768,3072]{1,0:T(8,128)(2,1)} %wo.1, bf16[3072,3072]{1,0:T(8,128)(2,1)} %wd.1), custom_call_target="tpu_custom_call" | custom-call | flops 3623878656 | bytes 56623104 | tf_op jit(solution)/shard_map/pallas_call | solution.py:253
  40.4 1.4 %copy.9 = bf16[8,3072]{1,0:T(8,128)(2,1)} copy(bf16[8,3072]{1,0:T(8,128)(2,1)} %shard_map.73) | data formatting | bytes 98304

commit v4 on v3

--- a/solution.py
+++ b/solution.py
@@ -83,12 +83,14 @@
             device_id=to, device_id_type=MESH,
         )
 
-    sends = [block(me, 0, y_peer)]
-    for step in range(1, lines):
+    order = sorted(range(1, lines), key=lambda step: min(step, lines - step))
+    sends = []
+    for step in order:
         sends.append(block(me, step, {"fin": line_at(step) * PAIR + y}))
+    sends.append(block(me, 0, y_peer))
     for send in sends:
         send.start()
-    for step in range(1, lines):
+    for step in order:
         source = line_at(lines - step) * PAIR + y
         passed = block(source, lines - 1 + step, y_peer)
         passed.wait_recv()

time: 42 us -> 41.4 us (0.986)
  Pallas kernels: 40.4 us -> 39.8 us
    pallas_call x1, Pallas kernels: 40.4 us -> 39.8 us  [fused(): pl.pallas_call(functools.partial(fused_kernel, lines, groups, chunks), ou...]
where the time goes in v4:
time: 41.4 us; the launch traced here: 41.2 us
  Pallas kernels  39.8 us (96%)
  local copies, waits for them, and re-layouts  1.42 us (3%)
    pallas_call x1, Pallas kernels, fused(): pl.pallas_call(functools.partial(fused_kernel, lines, groups, chunks), ou...  39.8 us
    unnamed x1, local copies, waits for them, and re-layouts  1.42 us

profile of v4, /device:TPU:0, one launch (start us, length us, event | category | flops | bytes accessed | tf_op | source)
XLA Modules:
  0.0 41.2 jit_solution(5323642826059185483)
XLA Ops:
  0.0 39.8 %shard_map.73 = bf16[8,3072]{1,0:T(8,128)(2,1)} custom-call(bf16[8,6144]{1,0:T(8,128)(2,1)} %tokens.1, s32[8]{0:T(128)} %ids.1, f32[1,6144]{1,0:T(1,128)} %bitcast.3, bf16[3,3072,768]{2,1,0:T(8,128)(2,1)} %bitcast.2, bf16[3072,3072]{1,0:T(8,128)(2,1)} %wu.1, bf16[768,3072]{1,0:T(8,128)(2,1)} %wo.1, bf16[3072,3072]{1,0:T(8,128)(2,1)} %wd.1), custom_call_target="tpu_custom_call" | custom-call | flops 3623878656 | bytes 56623104 | tf_op jit(solution)/shard_map/pallas_call | solution.py:255
  39.8 1.4 %copy.9 = bf16[8,3072]{1,0:T(8,128)(2,1)} copy(bf16[8,3072]{1,0:T(8,128)(2,1)} %shard_map.73) | data formatting | bytes 98304
